TPU v7x, 128 devices: a whole 4x4x4 slice. The times are simulated.
128 devices in a mesh: row: 16 (over z, x_hi, core), rep: 8 (over y, x_lo).
Axes of the slice: x: 4 (x_hi: 2, x_lo: 2; x = x_hi * 2 + x_lo), y: 4, z: 4, core: 2. Of those that a mesh axis runs over, the one named last changes fastest.
Arguments:
- features: float32 [131072, 128], P(('row', 'rep')), may hold values from -6 to 6
- weight: float32 [128, 128], replicated, may hold values from -0.5 to 0.5
- adjacency_tiles: float32 [40960, 128, 128], P(('row', 'rep')), may hold values from 0 to 0.05
- tile_rows: int32 [40960], P(('row', 'rep')), may hold values from 0 to 63
- tile_cols: int32 [40960], P(('row', 'rep')), may hold values from 0 to 127
- tile_counts: int32 [128], P(('row', 'rep')), may hold values from 1 to 320, as said below
- cluster_order: int32 [128, 1024], P(('row', 'rep')), may hold values from 0 to 1023, each once within a row
Outputs:
- activations: float32 [131072, 128], P(('row', 'rep'))
Inputs may be any that keep to these rules, and one draw needn't show every extreme that they name: `tile_counts`: every device has at least one live slot; some device fills all 320.
All inputs are finite; a program needn't handle non-finite values.
Results may differ from a plain program's by a relative error of at most 0.0003.
Values sent between devices are 32-bit elements; how exact they have to be, the bound alone decides.
A program may use at most 128 MiB of HBM per device.

v0:
```python
import jax
import jax.numpy as jnp
from jax import lax
from jax.sharding import PartitionSpec as P


def shards(features, weight, adjacency_tiles, tile_rows, tile_cols, tile_counts, cluster_order):
    ordered = jnp.take(features, cluster_order[0], axis=0)
    panels = lax.all_gather(ordered, "row", axis=0, tiled=True)
    panel_set = panels.reshape(-1, 128, panels.shape[1])
    picked = jnp.take(panel_set, tile_cols, axis=0)
    products = jnp.einsum("tij,tjf->tif", adjacency_tiles, picked, precision=lax.Precision.HIGHEST)
    slab_rows = features.shape[0]
    row_tiles = lax.axis_size("rep") * slab_rows // 128
    live_mask = (jnp.arange(adjacency_tiles.shape[0], dtype=jnp.int32) < tile_counts[0]).astype(
        products.dtype
    )
    products = products * live_mask[:, None, None]
    tile_sums = jax.ops.segment_sum(products, tile_rows, num_segments=row_tiles)
    partial_value = tile_sums.reshape(row_tiles * 128, products.shape[2])
    totals = lax.psum(partial_value, "rep")
    own_rows = lax.dynamic_slice_in_dim(totals, lax.axis_index("rep") * slab_rows, slab_rows, 0)
    mixed = jnp.dot(
        own_rows, weight, precision=lax.Precision.HIGHEST, preferred_element_type=jnp.float32
    )
    return jnp.maximum(mixed, 0.0)


def solution(mesh):
    placed = (
        P(("row", "rep"), None),
        P(),
        P(("row", "rep"), None, None),
        P(("row", "rep")),
        P(("row", "rep")),
        P(("row", "rep")),
        P(("row", "rep"), None),
    )
    return jax.shard_map(
        shards, mesh=mesh, in_specs=placed, out_specs=P(("row", "rep"), None), check_vma=False
    )
```

profile of v0, /device:TPU:0, one launch (start us, length us, event | category | flops | bytes accessed | tf_op | source)
XLA Modules:
  0.0 426.9 jit_solution(17014220164775437526)
XLA Ops:
  6.5 0.0 copy-start
  6.5 0.0 all-gather.2.cloned.1.call-start
  6.5 0.7 compare_select_fusion
  7.3 0.7 compare_and_fusion
  8.0 0.0 copy-done
  8.0 2.8 gather_fusion
  10.8 1.0 broadcast_select_fusion
  11.8 0.0 all-gather.2.cloned.1.call-update
  11.8 0.0 all-reduce.2.cloned.1.call-start
  12.5 0.7 compare_select_fusion.2
  13.2 0.7 fusion.7
  13.9 73.7 %all-gather.2.cloned.1.call-done = f32[16384,128]{1,0:T(8,128)} async-done(((f32[1024,128]{1,0:T(8,128)}), f32[16384,128]{1,0:T(8,128)}) %all-gather.2.cloned.1.call-update) | async-done | bytes 8388624 | tf_op jit(solution)/shard_map/all_gather | solution.py:9
  87.6 17.2 %gather_fusion.1 = f32[320,128,128]{2,1,0:T(8,128)} fusion(f32[128,128,128]{2,1,0:T(8,128)} %bitcast.13, s32[1024]{0:T(1024)S(1)} %pad_clamp_fusion), kind=kCustom, calls=%fused_computation.1 | custom fusion | bytes 41944320 | tf_op jit(solution)/shard_map/jit(_take)/gather | solution.py:11
  104.8 43.1 %multiply_bitcast_fusion = f32[320,128,128]{1,2,0:T(8,128)} fusion(f32[320]{0:T(512)S(1)} %get-tuple-element.5, f32[320,128,128]{2,1,0:T(8,128)} %param.9, f32[320,128,128]{2,1,0:T(8,128)} %gather_fusion.1, pred[320]{0:T(512)(128)(4,1)S(1)} %get-tuple-element.6), kind=kOutput, calls=%fused_computation.3 | convolution fusion | flops 8063549440 | bytes 62916160 | tf_op jit(solution)/shard_map/tij,tjf->tif/dot_general | solution.py:12
  147.9 0.0 copy-start.3
  147.9 21.1 %copy.10 = f32[320,128,128]{2,1,0:T(8,128)} copy(f32[320,128,128]{1,2,0:T(8,128)} %multiply_bitcast_fusion) | data formatting | bytes 41943040 | tf_op jit(solution)/shard_map/mul | solution.py:18
  169.0 0.0 copy-start.1
  169.0 2.5 broadcast_in_dim.29
  171.5 0.0 copy-done.3
  171.5 0.0 copy-start.2
  171.5 65.4 %scatter_fusion = f32[64,128,128]{2,1,0:T(8,128)} fusion(f32[64,128,128]{2,1,0:T(8,128)} %broadcast_in_dim.29, s32[320]{0:T(512)S(1)} %copy-done.3, f32[320,128,128]{2,1,0:T(8,128)} %copy.10), kind=kCustom, calls=%fused_computation.2 | custom fusion | flops 5242880 | bytes 62915840 | tf_op jit(solution)/shard_map/scatter-add | solution.py:19
  236.9 0.0 all-reduce.2.cloned.1.call-update
  237.0 180.7 %all-reduce.2.cloned.1.call-done = f32[8192,128]{1,0:T(8,128)} async-done(((f32[8192,128]{1,0:T(8,128)}), f32[8192,128]{1,0:T(8,128)}) %all-reduce.2.cloned.1.call-update) | async-done | bytes 4194320 | tf_op jit(solution)/shard_map/psum | solution.py:21
  417.6 0.0 copy-done.2
  417.6 2.4 convolution_maximum_fusion
  420.0 0.0 copy-done.1
  (2 shorter events, 0.0 us)
Async XLA Ops:
  6.5 1.5 copy-start
  6.5 81.0 %all-gather.2.cloned.1.call-start = ((), (), s32[]{:S(2)}) async-start(), calls=%async_computation | async-start | bytes 8912896 | tf_op jit(solution)/shard_map/all_gather | solution.py:9
  11.8 405.8 %all-reduce.2.cloned.1.call-start = ((), (), s32[]{:S(2)}) async-start(), calls=%async_computation.1 | async-start | bytes 8388608 | tf_op jit(solution)/shard_map/psum | solution.py:21
  147.9 23.6 %copy-start.3 = (s32[320]{0:T(512)S(1)}, s32[320]{0:T(512)}, u32[]{:S(2)}) copy-start(s32[320]{0:T(512)} %param.10) | copy-start | bytes 3844
  169.0 251.1 %copy-start.1 = (f32[1024,128]{1,0:T(8,128)S(1)}, f32[1024,128]{1,0:T(8,128)}, u32[]{:S(2)}) copy-start(f32[1024,128]{1,0:T(8,128)} %param.7) | copy-start | bytes 1572868
  171.5 246.2 %copy-start.2 = (f32[128,128]{1,0:T(8,128)S(1)}, f32[128,128]{1,0:T(8,128)}, u32[]{:S(2)}) copy-start(f32[128,128]{1,0:T(8,128)} %param.8) | copy-start | bytes 196612
Sparse Core Ops, SparseCore 0:
  12.0 75.5 all-gather.1
  237.1 180.5 all-reduce.1
where the time goes:
time: 429 us; the launch traced here: 427 us
  waiting for transfers between devices  254 us (59%)
  other arithmetic  69.3 us (16%)
  matrix products  45.5 us (11%)
  local copies, waits for them, and re-layouts  43.6 us (10%)
  between operations  14.1 us (3%)
    psum x1, waiting for transfers between devices, shards(): totals = lax.psum(partial_value, 'rep')  181 us
    all_gather x1, waiting for transfers between devices, shards(): panels = lax.all_gather(ordered, 'row', axis=0, tiled=True)  73.7 us
    scatter-add x1, other arithmetic, shards(): tile_sums = jax.ops.segment_sum(products, tile_rows, num_segments=row_tiles)  65.4 us
    dot_general x1, matrix products, shards(): jnp.einsum('tij,tjf->tif', adjacency_tiles, picked, precision=lax.Precisi...  43.1 us
    mul x1, local copies, waits for them, and re-layouts, shards(): products = products * live_mask[:, None, None]  21.1 us
    gather x1, local copies, waits for them, and re-layouts, shards(): picked = jnp.take(panel_set, tile_cols, axis=0)  17.2 us
  transfers between devices with their start and end apart: 2, of which 2 were waited for; matrix products, arithmetic and copies ran while one was open for 0% of the time, Pallas kernels for 0%

commit v1 on v0

v1 whole, which is shorter than its diff:
```python
import functools

import jax
import jax.numpy as jnp
from jax import lax
from jax.experimental import pallas as pl
from jax.experimental.pallas import tpu as pltpu
from jax.sharding import PartitionSpec as P

MESH = pl.DeviceIdType.MESH
F32, BF16 = jnp.float32, jnp.bfloat16
T = 320
NB = 4
APIECE = 16
ASTAGE = 2
UNROLL = 40


def body(perm, pos, keep, cslot, codd, has, order, feat, weight, adj, out,
         recv, panels, aq, astage, cbuf, part, ropp, radj, rx, ordered, wb,
         g_recv, s_send, o_recv, a_recv, x_recv, a_sem):
    r, c = lax.axis_index("row"), lax.axis_index("rep")
    z, xh, kp = r // 4, (r // 2) % 2, r % 2
    y, xl = c // 2, c % 2
    zp, zm, z2 = (z + 1) % 4, (z + 3) % 4, (z + 2) % 4

    ZP = (zp * 4 + xh * 2 + kp, c)
    ZM = (zm * 4 + xh * 2 + kp, c)
    XP = (z * 4 + (1 - xh) * 2 + kp, c)
    SB = (z * 4 + xh * 2 + (1 - kp), c)
    YP = (r, ((y + 1) % 4) * 2 + xl)
    YM = (r, ((y + 3) % 4) * 2 + xl)
    XL = (r, y * 2 + (1 - xl))

    def slot(zz, xx, kk):
        return kk * 8 + zz * 2 + xx

    OWN, P0 = slot(z, xh, kp), slot(z, 1 - xh, kp)
    AP, AM, A2 = slot(zp, xh, kp), slot(zm, xh, kp), slot(z2, xh, kp)
    BP, BM, B2 = slot(zp, 1 - xh, kp), slot(zm, 1 - xh, kp), slot(z2, 1 - xh, kp)

    lane = lax.broadcasted_iota(jnp.int32, (128, 128), 1) < 64
    sends = []

    def remote(refs, target):
        k = len(sends)

        def make():
            src, dst, rsem = refs()
            return pltpu.make_async_remote_copy(
                src_ref=src, dst_ref=dst, send_sem=s_send.at[k], recv_sem=rsem,
                device_id=target, device_id_type=MESH)
        sends.append(make)
        make().start()

    def arrive(ref, rsem):
        pltpu.make_async_remote_copy(
            src_ref=ref, dst_ref=ref, send_sem=s_send.at[0], recv_sem=rsem,
            device_id=SB, device_id_type=MESH).wait_recv()

    def piece(h, s, b):
        return recv.at[h, s, pl.ds(b * 128, 128)]

    def give(h, s, b, *targets):
        for t in targets:
            remote(lambda: (piece(h, s, b), piece(h, s, b), g_recv.at[h, s, b]), t)

    def got(h, s, b):
        arrive(piece(h, s, b), g_recv.at[h, s, b])

    def convert(h, s):
        def unit(u, _):
            v = recv[h, s, pl.ds(pl.multiple_of(u * 128, 128), 128), :]
            hi = v.astype(BF16).astype(F32)
            lo = v - hi
            panels[h, s * 8 + u] = jnp.where(lane, hi, pltpu.roll(lo, 64, 1)).astype(BF16)
            panels[h, s * 8 + u + 4] = jnp.where(lane, pltpu.roll(hi, 64, 1), lo).astype(BF16)
            return 0
        lax.fori_loop(0, 4, unit, 0)

    def pack(h):
        for u in range(4):
            a = ordered[pl.ds(u * 128, 128), :]
            b = ordered[pl.ds((u + 4) * 128, 128), :]
            if h == 0:
                v = jnp.where(lane, a, pltpu.roll(b, 64, 1))
            else:
                v = jnp.where(lane, pltpu.roll(a, 64, 1), b)
            recv[h, OWN, pl.ds(u * 128, 128), :] = v

    def own_sends(h):
        for b in range(NB):
            give(h, OWN, b, XP, ZP, ZM, SB)

    def stage1(h, b):
        got(h, AM, b)
        if b < NB // 2:
            give(h, AM, b, ZP)
        got(h, AP, b)
        if b >= NB // 2:
            give(h, AP, b, ZM)
        got(h, P0, b)
        give(h, P0, b, ZP, ZM, SB)
        give(h, AM, b, SB)
        give(h, AP, b, SB)

    def stage2(h, b):
        got(h, A2, b)
        give(h, A2, b, XP, SB)
        got(h, BM, b)
        give(h, BM, b, SB)
        got(h, BP, b)
        give(h, BP, b, SB)

    def stage3(h, b):
        got(h, B2, b)
        give(h, B2, b, SB)

    def stage4(h):
        k = 1 - kp
        for s in (slot(z, xh, k), slot(z, 1 - xh, k), slot(zp, xh, k), slot(zm, xh, k),
                  slot(zp, 1 - xh, k), slot(zm, 1 - xh, k), slot(z2, xh, k), slot(z2, 1 - xh, k)):
            for b in range(NB):
                got(h, s, b)
            convert(h, s)

    def a_copy(p):
        return pltpu.make_async_copy(
            adj.at[pl.ds(p * APIECE, APIECE)], astage.at[p % ASTAGE], a_sem.at[p % ASTAGE])

    def a_piece(p):
        a_copy(p).wait()

        def tile(t, _):
            v = astage[p % ASTAGE, t]
            hi = v.astype(BF16)
            aq[p * APIECE + t, :, 0:128] = hi
            aq[p * APIECE + t, :, 128:256] = (v - hi.astype(F32)).astype(BF16)
            return 0
        lax.fori_loop(0, APIECE, tile, 0, unroll=2)
        if p + ASTAGE < T // APIECE:
            a_copy(p + ASTAGE).start()

    def compute(h, events):
        def step(i, acc):
            for u in range(UNROLL // 2):
                j = i * UNROLL + 2 * u
                w = panels[h, pos[j]]
                a0 = acc * keep[j] + jnp.dot(
                    aq[perm[j]], jnp.concatenate([w, w], 0), preferred_element_type=F32)
                w = panels[h, pos[j + 1]]
                acc = a0 * keep[j + 1] + jnp.dot(
                    aq[perm[j + 1]], jnp.concatenate([w, w], 0), preferred_element_type=F32)
                cbuf[i * (UNROLL // 2) + u] = jnp.where(lane, a0, acc) + pltpu.roll(
                    jnp.where(lane, acc, a0), 64, 1)
            for k, run in events.items():
                pl.when(i == k)(run)
            return acc
        lax.fori_loop(0, T // UNROLL, step, jnp.zeros((128, 128), F32))

    def emit(h, yo, j):
        def unit(u, _):
            e = ((yo * 2 + j) * 4 + u) * 2
            v, w = cbuf[cslot[e]], cbuf[cslot[e + 1]]
            v = jnp.where(codd[e] != 0, pltpu.roll(v, 64, 1), v) * has[e]
            w = jnp.where(codd[e + 1] != 0, w, pltpu.roll(w, 64, 1)) * has[e + 1]
            part[h, yo, j, pl.ds(pl.multiple_of(u * 128, 128), 128), :] = jnp.where(lane, v, w)
            return 0
        lax.fori_loop(0, 4, unit, 0)

    LOW, HIGH = pl.ds(0, 256), pl.ds(256, 256)

    def opp(h, j):
        emit(h, 0, j)
        remote(lambda: (part.at[h, 0, j, LOW], ropp.at[h, 0, j], o_recv.at[h, 0, j]), YP)
        remote(lambda: (part.at[h, 0, j, HIGH], ropp.at[h, 1, j], o_recv.at[h, 1, j]), YM)

    def adj_now(h, j):
        emit(h, 1, j)
        remote(lambda: (part.at[h, 1, j, HIGH], radj.at[h, 0, j, HIGH], a_recv.at[h, 0, j, 1]), YP)
        emit(h, 2, j)
        remote(lambda: (part.at[h, 2, j, LOW], radj.at[h, 1, j, LOW], a_recv.at[h, 1, j, 0]), YM)

    def adj_late(h, j):
        arrive(ropp.at[h, 0, j], o_recv.at[h, 0, j])
        part[h, 1, j, LOW] = part[h, 1, j, LOW] + ropp[h, 0, j]
        remote(lambda: (part.at[h, 1, j, LOW], radj.at[h, 0, j, LOW], a_recv.at[h, 0, j, 0]), YP)
        arrive(ropp.at[h, 1, j], o_recv.at[h, 1, j])
        part[h, 2, j, HIGH] = part[h, 2, j, HIGH] + ropp[h, 1, j]
        remote(lambda: (part.at[h, 2, j, HIGH], radj.at[h, 1, j, HIGH], a_recv.at[h, 1, j, 1]), YM)

    def own_sum(h, j, b):
        rows = (LOW, HIGH)[b]
        for d in range(2):
            arrive(radj.at[h, d, j, rows], a_recv.at[h, d, j, b])
        part[h, 3, j, rows] = part[h, 3, j, rows] + (radj[h, 0, j, rows] + radj[h, 1, j, rows])
        if j == 0:
            remote(lambda: (part.at[h, 3, 0, rows], rx.at[h, rows], x_recv.at[h, b]), XL)

    def final(h, b):
        rows = (LOW, HIGH)[b]
        arrive(rx.at[h, rows], x_recv.at[h, b])
        for u in (2 * b, 2 * b + 1):
            rr = pl.ds(u * 128, 128)
            v = part[h, 3, 1, rr] + rx[h, rr]
            hi = v.astype(BF16)
            lo = (v - hi.astype(F32)).astype(BF16)
            m = (jnp.dot(hi, wb[h, 0], preferred_element_type=F32)
                 + jnp.dot(lo, wb[h, 0], preferred_element_type=F32)
                 + jnp.dot(hi, wb[h, 1], preferred_element_type=F32))
            ra, rb = pl.ds(u * 128, 128), pl.ds((u + 4) * 128, 128)
            if h == 0:
                out[ra, :] = m[:, :128]
                out[rb, :] = m[:, 128:]
            else:
                out[ra, :] = jnp.maximum(out[ra, :] + m[:, :128], 0.0)
                out[rb, :] = jnp.maximum(out[rb, :] + m[:, 128:], 0.0)

    for p in range(ASTAGE):
        a_copy(p).start()
    barrier = pltpu.get_barrier_semaphore()
    around = (ZP, ZM, XP, SB, YP, YM, XL)
    for t in around:
        pl.semaphore_signal(barrier, inc=1, device_id=t, device_id_type=MESH)

    def take(i, _):
        for k in range(16):
            ordered[pl.ds(i * 16 + k, 1), :] = feat[pl.ds(order[i * 16 + k], 1), :]
        return 0
    lax.fori_loop(0, 64, take, 0)
    pack(0)
    pl.semaphore_wait(barrier, len(around))
    own_sends(0)
    pack(1)
    convert(0, OWN)
    convert(1, OWN)
    wb[...] = jnp.zeros_like(wb)
    for h in range(2):
        w = weight[pl.ds(h * 64, 64), :]
        hi = w.astype(BF16)
        for k, v in enumerate((hi, (w - hi.astype(F32)).astype(BF16))):
            wb[h, k, 0:64, 0:128] = v
            wb[h, k, 64:128, 128:256] = v

    pieces = list(range(T // APIECE))
    for p in pieces[:6]:
        a_piece(p)
    todo = pieces[6:]
    for b in range(NB):
        stage1(0, b)
        for p in todo[3 * b:3 * b + 3]:
            a_piece(p)
    for s in (P0, AM, AP):
        convert(0, s)
    for b in range(NB):
        stage2(0, b)
        for p in todo[12 + b:13 + b]:
            a_piece(p)
    own_sends(1)
    for s in (A2, BM, BP):
        convert(0, s)
    for b in range(NB):
        stage3(0, b)
    convert(0, B2)
    stage4(0)

    compute(0, {1 + 2 * b: functools.partial(stage1, 1, b) for b in range(NB)})
    for j in range(2):
        opp(0, j)
    for j in range(2):
        adj_now(0, j)
    for b in range(NB):
        stage2(1, b)
    for j in range(2):
        adj_late(0, j)
    for j in range(2):
        emit(0, 3, j)
    for s in (P0, AM, AP, A2, BM, BP):
        convert(1, s)
    for b in range(NB):
        stage3(1, b)
    convert(1, B2)
    stage4(1)

    compute(1, {})
    for j in range(2):
        opp(1, j)
    for j in range(2):
        adj_now(1, j)
    for b in (1, 0):
        own_sum(0, 0, b)
    for j in range(2):
        adj_late(1, j)
    for j in range(2):
        emit(1, 3, j)
    for b in (1, 0):
        own_sum(0, 1, b)
        final(0, b)
    for j in range(2):
        for b in (1, 0):
            own_sum(1, j, b)
    for b in (1, 0):
        final(1, b)
    for make in sends:
        make().wait_send()


N_SEND = 2 * (15 * NB + 14)


def shards(features, weight, adjacency_tiles, tile_rows, tile_cols, tile_counts, cluster_order):
    c = lax.axis_index("rep")
    y, xl = c // 2, c % 2
    j = jnp.arange(T, dtype=jnp.int32)
    dy, rx_, t = (tile_rows // 16 - y) % 4, (tile_rows // 8) % 2, tile_rows % 8
    yo = jnp.where(dy == 0, 3, jnp.where(dy == 1, 1, jnp.where(dy == 2, 0, 2)))
    rel = ((yo * 2 + (rx_ == xl)) * 4 + t % 4) * 2 + t // 4
    key = jnp.where(j < tile_counts[0], rel, 64)
    k = tile_cols // 8
    place = ((k % 2) * 8 + k // 2) * 8 + tile_cols % 8
    code = key * 65536 + place * 512 + j
    rank = jnp.sum((code[None, :] < code[:, None]).astype(jnp.int32), axis=1)
    code = jnp.sum(jnp.where(rank[:, None] == j[None, :], code[:, None], 0), axis=0)
    perm, pos, row = code % 512, (code // 512) % 128, code // 65536
    keep = jnp.concatenate([jnp.zeros((1,), F32), (row[1:] == row[:-1]).astype(F32)])
    upto = jnp.sum((key[None, :] <= jnp.arange(-1, 64, dtype=jnp.int32)[:, None]).astype(jnp.int32), axis=1)
    has = (upto[1:] > upto[:-1]).astype(F32)
    last = jnp.maximum(upto[1:] - 1, 0)
    smem = pl.BlockSpec(memory_space=pltpu.SMEM)
    vmem = pl.BlockSpec(memory_space=pltpu.VMEM)
    dma = pltpu.SemaphoreType.DMA
    return pl.pallas_call(
        body,
        out_shape=jax.ShapeDtypeStruct((1024, 128), F32),
        in_specs=[smem] * 7 + [vmem, vmem, pl.BlockSpec(memory_space=pl.ANY)],
        out_specs=vmem,
        scratch_shapes=[
            pltpu.VMEM((2, 16, 512, 128), F32),
            pltpu.VMEM((2, 128, 128, 128), BF16),
            pltpu.VMEM((T, 128, 256), BF16),
            pltpu.VMEM((ASTAGE, APIECE, 128, 128), F32),
            pltpu.VMEM((T // 2, 128, 128), F32),
            pltpu.VMEM((2, 4, 2, 512, 128), F32),
            pltpu.VMEM((2, 2, 2, 256, 128), F32),
            pltpu.VMEM((2, 2, 2, 512, 128), F32),
            pltpu.VMEM((2, 512, 128), F32),
            pltpu.VMEM((1024, 128), F32),
            pltpu.VMEM((2, 2, 128, 256), BF16),
            dma((2, 16, NB)),
            dma((N_SEND,)),
            dma((2, 2, 2)),
            dma((2, 2, 2, 2)),
            dma((2, 2)),
            dma((ASTAGE,)),
        ],
        compiler_params=pltpu.CompilerParams(
            collective_id=0, has_side_effects=True, vmem_limit_bytes=63 * 1024 * 1024),
    )(perm, pos, keep, last // 2, last % 2, has, cluster_order[0], features, weight, adjacency_tiles)


def solution(mesh):
    placed = (
        P(("row", "rep"), None),
        P(),
        P(("row", "rep"), None, None),
        P(("row", "rep")),
        P(("row", "rep")),
        P(("row", "rep")),
        P(("row", "rep"), None),
    )
    return jax.shard_map(
        shards, mesh=mesh, in_specs=placed, out_specs=P(("row", "rep"), None), check_vma=False
    )
```

time: 429 us -> 97.3 us (0.23)
  waiting for transfers between devices: 254 us -> 0 us
  Pallas kernels: 0 us -> 90.4 us
  other arithmetic: 69.3 us -> 3.89 us
  matrix products: 45.5 us -> 0 us
  local copies, waits for them, and re-layouts: 43.6 us -> 1.87 us
  between operations: 14.1 us -> 0.68 us
    psum x1 -> x0, waiting for transfers between devices: 181 us -> none  [shards(): totals = lax.psum(partial_value, 'rep')]
    pallas_call x0 -> x1, Pallas kernels: none -> 90.4 us  [shards(): pl.pallas_call(body, out_shape=jax.ShapeDtypeStruct((1024, 128), F32), in...]
    all_gather x1 -> x0, waiting for transfers between devices: 73.7 us -> none  [shards(): panels = lax.all_gather(ordered, 'row', axis=0, tiled=True)]
    scatter-add x1 -> x0, other arithmetic: 65.4 us -> none  [shards(): tile_sums = jax.ops.segment_sum(products, tile_rows, num_segments=row_tiles)]
    dot_general x2 -> x0, matrix products: 45.5 us -> none  [the longest x1 43.1 us: shards(): jnp.einsum('tij,tjf->tif', adjacency_tiles, picked, precision=lax.Precisi...]
    mul x1 -> x0, local copies, waits for them, and re-layouts: 21.1 us -> none  [shards(): products = products * live_mask[:, None, None]]
    gather x2 -> x0, local copies, waits for them, and re-layouts: 20 us -> none  [the longest x1 17.2 us: shards(): picked = jnp.take(panel_set, tile_cols, axis=0)]
  transfers between devices with their start and end apart: 2 -> 0, of which waited for: 2 -> 0; matrix products, arithmetic and copies ran while one was open for 0% -> 0% of each run, Pallas kernels for 0% -> 0%
where the time goes in v1:
time: 97.3 us; the launch traced here: 96.9 us
  Pallas kernels  90.4 us (93%)
  other arithmetic  3.89 us (4%)
  local copies, waits for them, and re-layouts  1.87 us (2%)
    pallas_call x1, Pallas kernels, shards(): pl.pallas_call(body, out_shape=jax.ShapeDtypeStruct((1024, 128), F32), in...  90.4 us

profile of v1, /device:TPU:0, one launch (start us, length us, event | category | flops | bytes accessed | tf_op | source)
XLA Modules:
  0.0 96.9 jit_solution(16900702021099850274)
XLA Ops:
  0.7 0.7 fusion.15
  1.4 0.2 convert_reduce_fusion.1
  1.6 0.6 compare_convert_fusion.has
  2.2 0.7 and_select_fusion
  2.8 0.2 convert_reduce_fusion
  3.0 0.2 select_reduce_fusion
  3.2 0.6 add_select_fusion
  3.8 0.1 slice_compare_fusion
  3.9 0.7 add_convert_fusion.keep
  4.6 90.4 %shard_map.73 = f32[1024,128]{1,0:T(8,128)} custom-call(s32[320]{0:T(512)} %get-tuple-element.8.perm, s32[320]{0:T(512)} %get-tuple-element.9.pos, f32[320]{0:T(512)} %add_convert_fusion.keep, s32[64]{0:T(128)} %get-tuple-element.11.cslot, s32[64]{0:T(128)} %get-tuple-element.10.codd, f32[64]{0:T(128)} %compare_convert_fusion.has, s32[1024]{0:T(1024)} %bitcast.3, ...), custom_call_target="tpu_custom_call" | custom-call | tf_op jit(solution)/shard_map/pallas_call | solution.py:332
  95.0 1.9 %copy.10 = f32[1024,128]{1,0:T(8,128)} copy(f32[1024,128]{1,0:T(8,128)} %shard_map.73) | data formatting | bytes 1048576
  (1 shorter events, 0.0 us)

commit v2 on v1

--- a/solution.py
+++ b/solution.py
@@ -12,13 +12,13 @@
 T = 320
 NB = 4
 APIECE = 16
-ASTAGE = 2
-UNROLL = 40
-
-
-def body(perm, pos, keep, cslot, codd, has, order, feat, weight, adj, out,
+ASTAGE = 4
+UNROLL = 64
+
+
+def body(order, code, feat, weight, adj, out,
          recv, panels, aq, astage, cbuf, part, ropp, radj, rx, ordered, wb,
-         g_recv, s_send, o_recv, a_recv, x_recv, a_sem):
+         ivec, fvec, itab, ftab, g_recv, s_send, o_recv, a_recv, x_recv, a_sem, t_sem):
     r, c = lax.axis_index("row"), lax.axis_index("rep")
     z, xh, kp = r // 4, (r // 2) % 2, r % 2
     y, xl = c // 2, c % 2
@@ -71,42 +71,48 @@
     def convert(h, s):
         def unit(u, _):
             v = recv[h, s, pl.ds(pl.multiple_of(u * 128, 128), 128), :]
-            hi = v.astype(BF16).astype(F32)
-            lo = v - hi
-            panels[h, s * 8 + u] = jnp.where(lane, hi, pltpu.roll(lo, 64, 1)).astype(BF16)
-            panels[h, s * 8 + u + 4] = jnp.where(lane, pltpu.roll(hi, 64, 1), lo).astype(BF16)
+            hi = v.astype(BF16)
+            panels[h, s * 4 + u, :, 0:128] = hi
+            panels[h, s * 4 + u, :, 128:256] = (v - hi.astype(F32)).astype(BF16)
             return 0
-        lax.fori_loop(0, 4, unit, 0)
-
-    def pack(h):
-        for u in range(4):
-            a = ordered[pl.ds(u * 128, 128), :]
-            b = ordered[pl.ds((u + 4) * 128, 128), :]
-            if h == 0:
-                v = jnp.where(lane, a, pltpu.roll(b, 64, 1))
-            else:
-                v = jnp.where(lane, pltpu.roll(a, 64, 1), b)
-            recv[h, OWN, pl.ds(u * 128, 128), :] = v
-
-    def own_sends(h):
-        for b in range(NB):
-            give(h, OWN, b, XP, ZP, ZM, SB)
-
-    def stage1(h, b):
+        lax.fori_loop(0, 4, unit, 0, unroll=2)
+
+    def pack(h, u):
+        a = ordered[pl.ds(u * 128, 128), :]
+        b = ordered[pl.ds((u + 4) * 128, 128), :]
+        if h == 0:
+            v = jnp.where(lane, a, pltpu.roll(b, 64, 1))
+        else:
+            v = jnp.where(lane, pltpu.roll(a, 64, 1), b)
+        recv[h, OWN, pl.ds(u * 128, 128), :] = v
+
+    def own_sends(h, b):
+        give(h, OWN, b, (ZP, ZM)[b % 2], XP, SB)
+        if b == NB - 1:
+            for k in range(NB):
+                give(h, OWN, k, (ZM, ZP)[k % 2])
+
+    def relay(h, b):
         got(h, AM, b)
-        if b < NB // 2:
-            give(h, AM, b, ZP)
-        got(h, AP, b)
-        if b >= NB // 2:
-            give(h, AP, b, ZM)
+        give(h, AM, b, ZP, SB)
+        got(h, AP, b + 1)
+        give(h, AP, b + 1, ZM, SB)
+
+    def across(h, b):
         got(h, P0, b)
         give(h, P0, b, ZP, ZM, SB)
-        give(h, AM, b, SB)
+
+    def rest(h, b):
+        got(h, AM, b + 1)
+        give(h, AM, b + 1, SB)
+        got(h, AP, b)
         give(h, AP, b, SB)
 
     def stage2(h, b):
         got(h, A2, b)
         give(h, A2, b, XP, SB)
+
+    def stage2b(h, b):
         got(h, BM, b)
         give(h, BM, b, SB)
         got(h, BP, b)
@@ -119,7 +125,7 @@
     def stage4(h):
         k = 1 - kp
         for s in (slot(z, xh, k), slot(z, 1 - xh, k), slot(zp, xh, k), slot(zm, xh, k),
-                  slot(zp, 1 - xh, k), slot(zm, 1 - xh, k), slot(z2, xh, k), slot(z2, 1 - xh, k)):
+                  slot(z2, xh, k), slot(zp, 1 - xh, k), slot(zm, 1 - xh, k), slot(z2, 1 - xh, k)):
             for b in range(NB):
                 got(h, s, b)
             convert(h, s)
@@ -142,16 +148,22 @@
             a_copy(p + ASTAGE).start()
 
     def compute(h, events):
+        low = lax.broadcasted_iota(jnp.int32, (1, 128), 1) < 64
+
         def step(i, acc):
-            for u in range(UNROLL // 2):
-                j = i * UNROLL + 2 * u
-                w = panels[h, pos[j]]
-                a0 = acc * keep[j] + jnp.dot(
-                    aq[perm[j]], jnp.concatenate([w, w], 0), preferred_element_type=F32)
-                w = panels[h, pos[j + 1]]
-                acc = a0 * keep[j + 1] + jnp.dot(
-                    aq[perm[j + 1]], jnp.concatenate([w, w], 0), preferred_element_type=F32)
-                cbuf[i * (UNROLL // 2) + u] = jnp.where(lane, a0, acc) + pltpu.roll(
+            row, col = i // (128 // UNROLL), (i % (128 // UNROLL)) * UNROLL
+
+            def add(u, acc):
+                w = panels[h, itab[3 + row, col + u]]
+                p = jnp.dot(aq[itab[row, col + u]], jnp.concatenate([w, w], 0),
+                            preferred_element_type=F32)
+                side = jnp.where(low, ftab[3 + row, col + u], ftab[6 + row, col + u])
+                return acc * ftab[row, col + u] + (p[:, :128] + p[:, 128:]) * side
+
+            for u in range(0, UNROLL, 2):
+                a0 = add(u, acc)
+                acc = add(u + 1, a0)
+                cbuf[i * (UNROLL // 2) + u // 2] = jnp.where(lane, a0, acc) + pltpu.roll(
                     jnp.where(lane, acc, a0), 64, 1)
             for k, run in events.items():
                 pl.when(i == k)(run)
@@ -159,14 +171,48 @@
         lax.fori_loop(0, T // UNROLL, step, jnp.zeros((128, 128), F32))
 
     def emit(h, yo, j):
+        low = lax.broadcasted_iota(jnp.int32, (1, 128), 1) < 64
+
         def unit(u, _):
             e = ((yo * 2 + j) * 4 + u) * 2
-            v, w = cbuf[cslot[e]], cbuf[cslot[e + 1]]
-            v = jnp.where(codd[e] != 0, pltpu.roll(v, 64, 1), v) * has[e]
-            w = jnp.where(codd[e + 1] != 0, w, pltpu.roll(w, 64, 1)) * has[e + 1]
-            part[h, yo, j, pl.ds(pl.multiple_of(u * 128, 128), 128), :] = jnp.where(lane, v, w)
+            v, w = cbuf[itab[6, e]], cbuf[itab[6, e + 1]]
+            stay = jnp.where(low, ftab[9, e], ftab[10, e + 1])
+            turn = jnp.where(low, ftab[10, e], ftab[9, e + 1])
+            part[h, yo, j, pl.ds(pl.multiple_of(u * 128, 128), 128), :] = (
+                jnp.where(lane, v, w) * stay + pltpu.roll(jnp.where(lane, w, v), 64, 1) * turn)
             return 0
-        lax.fori_loop(0, 4, unit, 0)
+        lax.fori_loop(0, 4, unit, 0, unroll=4)
+
+    def tables():
+        def down(v):
+            return jnp.transpose(jnp.broadcast_to(v, (128, 128)))
+
+        def total(v):
+            return jnp.sum(v, axis=0, keepdims=True)
+        at = lax.broadcasted_iota(jnp.int32, (1, 128), 1)
+        rows = [code[pl.ds(k, 1), :] for k in range(3)]
+        cols = [down(v) for v in rows]
+        ranks = [down(sum(total((m < v).astype(jnp.int32)) for m in cols)) for v in rows]
+        for k in range(3):
+            here = sum(total(jnp.where(n == at + k * 128, m, 0)) for n, m in zip(ranks, cols))
+            back = sum(total(jnp.where(n == at + (k * 128 - 1), m, 0)) for n, m in zip(ranks, cols))
+            side = (here // 32768) % 2
+            ivec[pl.ds(k, 1), :] = jnp.minimum(here % 512, T - 1)
+            ivec[pl.ds(3 + k, 1), :] = (here // 512) % 64
+            fvec[pl.ds(k, 1), :] = (here // 65536 == back // 65536).astype(F32)
+            fvec[pl.ds(3 + k, 1), :] = (1 - side).astype(F32)
+            fvec[pl.ds(6 + k, 1), :] = side.astype(F32)
+        upto = sum(total((m // 65536 <= at).astype(jnp.int32)) for m in cols)
+        before = sum(total((m // 65536 < at).astype(jnp.int32)) for m in cols)
+        last = jnp.clip(upto - 1, 0, T - 1)
+        has = jnp.where(upto > before, 1, 0)
+        ivec[pl.ds(6, 1), :] = last // 2
+        fvec[pl.ds(9, 1), :] = (has * (1 - last % 2)).astype(F32)
+        fvec[pl.ds(10, 1), :] = (has * (last % 2)).astype(F32)
+
+    def table_copies():
+        return (pltpu.make_async_copy(ivec, itab, t_sem.at[0]),
+                pltpu.make_async_copy(fvec, ftab, t_sem.at[1]))
 
     LOW, HIGH = pl.ds(0, 256), pl.ds(256, 256)
 
@@ -216,24 +262,52 @@
                 out[ra, :] = jnp.maximum(out[ra, :] + m[:, :128], 0.0)
                 out[rb, :] = jnp.maximum(out[rb, :] + m[:, 128:], 0.0)
 
-    for p in range(ASTAGE):
-        a_copy(p).start()
     barrier = pltpu.get_barrier_semaphore()
     around = (ZP, ZM, XP, SB, YP, YM, XL)
     for t in around:
         pl.semaphore_signal(barrier, inc=1, device_id=t, device_id_type=MESH)
-
-    def take(i, _):
-        for k in range(16):
-            ordered[pl.ds(i * 16 + k, 1), :] = feat[pl.ds(order[i * 16 + k], 1), :]
-        return 0
-    lax.fori_loop(0, 64, take, 0)
-    pack(0)
-    pl.semaphore_wait(barrier, len(around))
-    own_sends(0)
-    pack(1)
-    convert(0, OWN)
-    convert(1, OWN)
+    for p in range(ASTAGE):
+        a_copy(p).start()
+
+    for u in range(NB):
+        for o in (u, u + 4):
+            def take(i, _):
+                for k in range(16):
+                    at = o * 128 + i * 16 + k
+                    ordered[pl.ds(at, 1), :] = feat[pl.ds(order[0, at], 1), :]
+                return 0
+            lax.fori_loop(0, 8, take, 0)
+        pack(0, u)
+        if u == 0:
+            pl.semaphore_wait(barrier, len(around))
+        own_sends(0, u)
+    ivec[...] = jnp.zeros_like(ivec)
+    fvec[...] = jnp.zeros_like(fvec)
+    tables()
+    for copy in table_copies():
+        copy.start()
+
+    todo = iter(range(T // APIECE))
+
+    def a_pieces(n):
+        for _ in range(n):
+            p = next(todo, None)
+            if p is not None:
+                a_piece(p)
+
+    a_pieces(2)
+    relay(0, 0)
+    a_pieces(2)
+    across(0, 0)
+    relay(0, 2)
+    a_pieces(2)
+    for b in range(1, NB):
+        across(0, b)
+        a_pieces(1)
+    for u in range(4):
+        pack(1, u)
+    for h in range(2):
+        convert(h, OWN)
     wb[...] = jnp.zeros_like(wb)
     for h in range(2):
         w = weight[pl.ds(h * 64, 64), :]
@@ -241,33 +315,43 @@
         for k, v in enumerate((hi, (w - hi.astype(F32)).astype(BF16))):
             wb[h, k, 0:64, 0:128] = v
             wb[h, k, 64:128, 128:256] = v
-
-    pieces = list(range(T // APIECE))
-    for p in pieces[:6]:
-        a_piece(p)
-    todo = pieces[6:]
-    for b in range(NB):
-        stage1(0, b)
-        for p in todo[3 * b:3 * b + 3]:
-            a_piece(p)
-    for s in (P0, AM, AP):
+    for b in (0, 2):
+        rest(0, b)
+        a_pieces(1)
+    for b in range(NB):
+        stage2(0, b)
+        a_pieces(1)
+    for s in (P0, AM, AP, A2):
         convert(0, s)
-    for b in range(NB):
-        stage2(0, b)
-        for p in todo[12 + b:13 + b]:
-            a_piece(p)
-    own_sends(1)
-    for s in (A2, BM, BP):
+        a_pieces(1)
+    for b in range(NB):
+        stage2b(0, b)
+        own_sends(1, b)
+        a_pieces(1)
+    for s in (BM, BP):
         convert(0, s)
     for b in range(NB):
         stage3(0, b)
     convert(0, B2)
+    for copy in table_copies():
+        copy.wait()
     stage4(0)
 
-    compute(0, {1 + 2 * b: functools.partial(stage1, 1, b) for b in range(NB)})
+    def both(*runs):
+        def go():
+            for f, *args in runs:
+                f(*args)
+        return go
+
+    compute(0, {
+        0: both((relay, 1, 0)),
+        1: both((across, 1, 0), (relay, 1, 2)),
+        2: both((across, 1, 1)),
+        3: both((across, 1, 2), (rest, 1, 0)),
+        4: both((across, 1, 3), (rest, 1, 2)),
+    })
     for j in range(2):
         opp(0, j)
-    for j in range(2):
         adj_now(0, j)
     for b in range(NB):
         stage2(1, b)
@@ -275,27 +359,33 @@
         adj_late(0, j)
     for j in range(2):
         emit(0, 3, j)
-    for s in (P0, AM, AP, A2, BM, BP):
+    for s in (P0, AM, AP, A2):
+        convert(1, s)
+    for b in range(NB):
+        stage2b(1, b)
+    for s in (BM, BP):
         convert(1, s)
     for b in range(NB):
         stage3(1, b)
     convert(1, B2)
     stage4(1)
 
-    compute(1, {})
-    for j in range(2):
-        opp(1, j)
-    for j in range(2):
-        adj_now(1, j)
-    for b in (1, 0):
-        own_sum(0, 0, b)
-    for j in range(2):
-        adj_late(1, j)
-    for j in range(2):
-        emit(1, 3, j)
+    compute(1, {
+        3: both((own_sum, 0, 0, 1)),
+        4: both((own_sum, 0, 0, 0)),
+    })
+    opp(1, 0)
+    adj_now(1, 0)
+    opp(1, 1)
+    adj_now(1, 1)
+    emit(1, 3, 0)
+    emit(1, 3, 1)
     for b in (1, 0):
         own_sum(0, 1, b)
+    adj_late(1, 0)
+    for b in (1, 0):
         final(0, b)
+    adj_late(1, 1)
     for j in range(2):
         for b in (1, 0):
             own_sum(1, j, b)
@@ -316,27 +406,22 @@
     yo = jnp.where(dy == 0, 3, jnp.where(dy == 1, 1, jnp.where(dy == 2, 0, 2)))
     rel = ((yo * 2 + (rx_ == xl)) * 4 + t % 4) * 2 + t // 4
     key = jnp.where(j < tile_counts[0], rel, 64)
-    k = tile_cols // 8
-    place = ((k % 2) * 8 + k // 2) * 8 + tile_cols % 8
-    code = key * 65536 + place * 512 + j
-    rank = jnp.sum((code[None, :] < code[:, None]).astype(jnp.int32), axis=1)
-    code = jnp.sum(jnp.where(rank[:, None] == j[None, :], code[:, None], 0), axis=0)
-    perm, pos, row = code % 512, (code // 512) % 128, code // 65536
-    keep = jnp.concatenate([jnp.zeros((1,), F32), (row[1:] == row[:-1]).astype(F32)])
-    upto = jnp.sum((key[None, :] <= jnp.arange(-1, 64, dtype=jnp.int32)[:, None]).astype(jnp.int32), axis=1)
-    has = (upto[1:] > upto[:-1]).astype(F32)
-    last = jnp.maximum(upto[1:] - 1, 0)
+    k, o = tile_cols // 8, tile_cols % 8
+    panel = ((k % 2) * 8 + k // 2) * 4 + o % 4
+    code = key * 65536 + (o // 4) * 32768 + panel * 512 + j
+    more = jnp.arange(T, 384, dtype=jnp.int32) + 64 * 65536
+    code = jnp.concatenate([code, more]).reshape(3, 128)
     smem = pl.BlockSpec(memory_space=pltpu.SMEM)
     vmem = pl.BlockSpec(memory_space=pltpu.VMEM)
     dma = pltpu.SemaphoreType.DMA
     return pl.pallas_call(
         body,
         out_shape=jax.ShapeDtypeStruct((1024, 128), F32),
-        in_specs=[smem] * 7 + [vmem, vmem, pl.BlockSpec(memory_space=pl.ANY)],
+        in_specs=[smem, vmem, vmem, vmem, pl.BlockSpec(memory_space=pl.ANY)],
         out_specs=vmem,
         scratch_shapes=[
             pltpu.VMEM((2, 16, 512, 128), F32),
-            pltpu.VMEM((2, 128, 128, 128), BF16),
+            pltpu.VMEM((2, 64, 128, 256), BF16),
             pltpu.VMEM((T, 128, 256), BF16),
             pltpu.VMEM((ASTAGE, APIECE, 128, 128), F32),
             pltpu.VMEM((T // 2, 128, 128), F32),
@@ -346,16 +431,21 @@
             pltpu.VMEM((2, 512, 128), F32),
             pltpu.VMEM((1024, 128), F32),
             pltpu.VMEM((2, 2, 128, 256), BF16),
+            pltpu.VMEM((16, 128), jnp.int32),
+            pltpu.VMEM((16, 128), F32),
+            pltpu.SMEM((16, 128), jnp.int32),
+            pltpu.SMEM((16, 128), F32),
             dma((2, 16, NB)),
             dma((N_SEND,)),
             dma((2, 2, 2)),
             dma((2, 2, 2, 2)),
             dma((2, 2)),
             dma((ASTAGE,)),
+            dma((2,)),
         ],
         compiler_params=pltpu.CompilerParams(
             collective_id=0, has_side_effects=True, vmem_limit_bytes=63 * 1024 * 1024),
-    )(perm, pos, keep, last // 2, last % 2, has, cluster_order[0], features, weight, adjacency_tiles)
+    )(cluster_order, code, features, weight, adjacency_tiles)
 
 
 def solution(mesh):

time: 97.3 us -> 87.4 us (0.90)
  Pallas kernels: 90.4 us -> 83.2 us
  other arithmetic: 3.89 us -> 1.39 us
    pallas_call x1, Pallas kernels: 90.4 us -> 83.2 us  [shards(): pl.pallas_call(body, out_shape=jax.ShapeDtypeStruct((1024, 128), F32), in...]
    select_n x2 -> x0, other arithmetic: 1.27 us -> none  [the longest x1 0.66 us: shards(): last % 2]
where the time goes in v2:
time: 87.4 us; the launch traced here: 87.1 us
  Pallas kernels  83.2 us (95%)
  local copies, waits for them, and re-layouts  1.87 us (2%)
  other arithmetic  1.39 us (2%)
    pallas_call x1, Pallas kernels, shards(): pl.pallas_call(body, out_shape=jax.ShapeDtypeStruct((1024, 128), F32), in...  83.2 us
    unnamed x1, local copies, waits for them, and re-layouts  1.87 us

profile of v2, /device:TPU:0, one launch (start us, length us, event | category | flops | bytes accessed | tf_op | source)
XLA Modules:
  0.0 87.1 jit_solution(3308552354938868081)
XLA Ops:
  0.7 0.7 fusion.12
  1.4 0.7 add_bitcast_fusion.code
  2.0 83.2 %shard_map.73 = f32[1024,128]{1,0:T(8,128)} custom-call(s32[1,1024]{1,0:T(1,128)} %order.1, s32[3,128]{1,0:T(4,128)} %add_bitcast_fusion.code, f32[1024,128]{1,0:T(8,128)} %feat.1, f32[128,128]{1,0:T(8,128)} %weight.1, f32[320,128,128]{2,1,0:T(8,128)} %adj.1), custom_call_target="tpu_custom_call" | custom-call | tf_op jit(solution)/shard_map/pallas_call | solution.py:417
  85.3 1.9 %copy.10 = f32[1024,128]{1,0:T(8,128)} copy(f32[1024,128]{1,0:T(8,128)} %shard_map.73) | data formatting | bytes 1048576
  (1 shorter events, 0.0 us)

commit v3 on v2

--- a/solution.py
+++ b/solution.py
@@ -14,11 +14,12 @@
 APIECE = 16
 ASTAGE = 4
 UNROLL = 64
+FY = 384
 
 
 def body(order, code, feat, weight, adj, out,
-         recv, panels, aq, astage, cbuf, part, ropp, radj, rx, ordered, wb,
-         ivec, fvec, itab, ftab, g_recv, s_send, o_recv, a_recv, x_recv, a_sem, t_sem):
+         recv, panels, aq, astage, cbuf, part, first, ropp, radj, rx, ordered, wb,
+         ivec, fvec, itab, ftab, g_recv, c_recv, s_send, f_recv, o_recv, a_recv, x_recv, a_sem, t_sem):
     r, c = lax.axis_index("row"), lax.axis_index("rep")
     z, xh, kp = r // 4, (r // 2) % 2, r % 2
     y, xl = c // 2, c % 2
@@ -40,33 +41,31 @@
     BP, BM, B2 = slot(zp, 1 - xh, kp), slot(zm, 1 - xh, kp), slot(z2, 1 - xh, kp)
 
     lane = lax.broadcasted_iota(jnp.int32, (128, 128), 1) < 64
-    sends = []
-
-    def remote(refs, target):
-        k = len(sends)
-
-        def make():
-            src, dst, rsem = refs()
-            return pltpu.make_async_remote_copy(
-                src_ref=src, dst_ref=dst, send_sem=s_send.at[k], recv_sem=rsem,
-                device_id=target, device_id_type=MESH)
-        sends.append(make)
-        make().start()
+    def remote(src, dst, ssem, rsem, target):
+        pltpu.make_async_remote_copy(
+            src_ref=src, dst_ref=dst, send_sem=ssem, recv_sem=rsem,
+            device_id=target, device_id_type=MESH).start()
 
     def arrive(ref, rsem):
         pltpu.make_async_remote_copy(
             src_ref=ref, dst_ref=ref, send_sem=s_send.at[0], recv_sem=rsem,
             device_id=SB, device_id_type=MESH).wait_recv()
 
+    def sent(ref, ssem):
+        pltpu.make_async_remote_copy(
+            src_ref=ref, dst_ref=ref, send_sem=ssem, recv_sem=f_recv.at[0],
+            device_id=SB, device_id_type=MESH).wait_send()
+
     def piece(h, s, b):
         return recv.at[h, s, pl.ds(b * 128, 128)]
 
     def give(h, s, b, *targets):
         for t in targets:
-            remote(lambda: (piece(h, s, b), piece(h, s, b), g_recv.at[h, s, b]), t)
+            there = c_recv.at[h, s % 8] if t is SB else g_recv.at[h, s % 8, b]
+            remote(piece(h, s, b), piece(h, s, b), s_send.at[h], there, t)
 
     def got(h, s, b):
-        arrive(piece(h, s, b), g_recv.at[h, s, b])
+        arrive(piece(h, s, b), g_recv.at[h, s % 8, b])
 
     def convert(h, s):
         def unit(u, _):
@@ -86,11 +85,22 @@
             v = jnp.where(lane, pltpu.roll(a, 64, 1), b)
         recv[h, OWN, pl.ds(u * 128, 128), :] = v
 
-    def own_sends(h, b):
-        give(h, OWN, b, (ZP, ZM)[b % 2], XP, SB)
-        if b == NB - 1:
-            for k in range(NB):
-                give(h, OWN, k, (ZM, ZP)[k % 2])
+    def start(h):
+        for b in (0, 2):
+            give(h, OWN, b, ZP)
+            give(h, OWN, b + 1, ZM)
+        for b in (0, 1):
+            give(h, OWN, b, XP)
+
+    def more(h):
+        for b in (2, 3):
+            give(h, OWN, b, XP)
+        for b in range(NB):
+            give(h, OWN, b, SB)
+
+    def fill(h, b):
+        give(h, OWN, b + 1, ZP)
+        give(h, OWN, b, ZM)
 
     def relay(h, b):
         got(h, AM, b)
@@ -126,8 +136,7 @@
         k = 1 - kp
         for s in (slot(z, xh, k), slot(z, 1 - xh, k), slot(zp, xh, k), slot(zm, xh, k),
                   slot(z2, xh, k), slot(zp, 1 - xh, k), slot(zm, 1 - xh, k), slot(z2, 1 - xh, k)):
-            for b in range(NB):
-                got(h, s, b)
+            arrive(recv.at[h, s], c_recv.at[h, s % 8])
             convert(h, s)
 
     def a_copy(p):
@@ -170,18 +179,15 @@
             return acc
         lax.fori_loop(0, T // UNROLL, step, jnp.zeros((128, 128), F32))
 
-    def emit(h, yo, j):
+    def emit(h, yo, j, units=range(4)):
         low = lax.broadcasted_iota(jnp.int32, (1, 128), 1) < 64
-
-        def unit(u, _):
+        for u in units:
             e = ((yo * 2 + j) * 4 + u) * 2
             v, w = cbuf[itab[6, e]], cbuf[itab[6, e + 1]]
             stay = jnp.where(low, ftab[9, e], ftab[10, e + 1])
             turn = jnp.where(low, ftab[10, e], ftab[9, e + 1])
-            part[h, yo, j, pl.ds(pl.multiple_of(u * 128, 128), 128), :] = (
+            part[h, yo, j, pl.ds(u * 128, 128), :] = (
                 jnp.where(lane, v, w) * stay + pltpu.roll(jnp.where(lane, w, v), 64, 1) * turn)
-            return 0
-        lax.fori_loop(0, 4, unit, 0, unroll=4)
 
     def tables():
         def down(v):
@@ -214,41 +220,73 @@
         return (pltpu.make_async_copy(ivec, itab, t_sem.at[0]),
                 pltpu.make_async_copy(fvec, ftab, t_sem.at[1]))
 
-    LOW, HIGH = pl.ds(0, 256), pl.ds(256, 256)
-
-    def opp(h, j):
-        emit(h, 0, j)
-        remote(lambda: (part.at[h, 0, j, LOW], ropp.at[h, 0, j], o_recv.at[h, 0, j]), YP)
-        remote(lambda: (part.at[h, 0, j, HIGH], ropp.at[h, 1, j], o_recv.at[h, 1, j]), YM)
-
-    def adj_now(h, j):
-        emit(h, 1, j)
-        remote(lambda: (part.at[h, 1, j, HIGH], radj.at[h, 0, j, HIGH], a_recv.at[h, 0, j, 1]), YP)
-        emit(h, 2, j)
-        remote(lambda: (part.at[h, 2, j, LOW], radj.at[h, 1, j, LOW], a_recv.at[h, 1, j, 0]), YM)
+    LATE = pl.ds(FY, 512 - FY)
+
+    def half(j, b):
+        n = FY // 2 if j < 2 else (512 - FY) // 2
+        return min(j, 1), pl.ds((FY if j == 2 else 0) + b * n, n), pl.ds(0, n)
+
+    def first_x(h):
+        for yo in range(4):
+            emit(h, yo, 0, range(FY // 128, 4))
+        remote(part.at[h, :, 0, LATE], first.at[h], s_send.at[2 + h], f_recv.at[h], XL)
+
+    def first_add(h):
+        arrive(first.at[h], f_recv.at[h])
+        for yo in range(4):
+            part[h, yo, 1, LATE] = part[h, yo, 1, LATE] + first[h, yo]
+        now(h, 2)
+
+    def adj_send(h, j, d, b):
+        k, rows, _ = half(j, b)
+        remote(part.at[h, 1 + d, k, rows], radj.at[h, d, k, rows],
+               s_send.at[2 + h], a_recv.at[h, d, j, b], (YP, YM)[d])
+
+    def now(h, j):
+        for d in range(2):
+            k, rows, there = half(j, d)
+            if j < 2:
+                emit(h, 0, k, range(0 if d == 0 else 2, 2 if d == 0 else 3))
+            remote(part.at[h, 0, k, rows], ropp.at[h, d, j, there],
+                   s_send.at[2 + h], o_recv.at[h, d, j], (YP, YM)[d])
+        for d in range(2):
+            if j < 2:
+                emit(h, 1 + d, k, range(FY // 128))
+            adj_send(h, j, d, 1 - d)
 
     def adj_late(h, j):
-        arrive(ropp.at[h, 0, j], o_recv.at[h, 0, j])
-        part[h, 1, j, LOW] = part[h, 1, j, LOW] + ropp[h, 0, j]
-        remote(lambda: (part.at[h, 1, j, LOW], radj.at[h, 0, j, LOW], a_recv.at[h, 0, j, 0]), YP)
-        arrive(ropp.at[h, 1, j], o_recv.at[h, 1, j])
-        part[h, 2, j, HIGH] = part[h, 2, j, HIGH] + ropp[h, 1, j]
-        remote(lambda: (part.at[h, 2, j, HIGH], radj.at[h, 1, j, HIGH], a_recv.at[h, 1, j, 1]), YM)
-
-    def own_sum(h, j, b):
-        rows = (LOW, HIGH)[b]
         for d in range(2):
-            arrive(radj.at[h, d, j, rows], a_recv.at[h, d, j, b])
-        part[h, 3, j, rows] = part[h, 3, j, rows] + (radj[h, 0, j, rows] + radj[h, 1, j, rows])
-        if j == 0:
-            remote(lambda: (part.at[h, 3, 0, rows], rx.at[h, rows], x_recv.at[h, b]), XL)
-
-    def final(h, b):
-        rows = (LOW, HIGH)[b]
-        arrive(rx.at[h, rows], x_recv.at[h, b])
-        for u in (2 * b, 2 * b + 1):
+            k, rows, there = half(j, d)
+            arrive(ropp.at[h, d, j, there], o_recv.at[h, d, j])
+            part[h, 1 + d, k, rows] = part[h, 1 + d, k, rows] + ropp[h, d, j, there]
+            adj_send(h, j, d, d)
+
+    def own_sum(h, j):
+        for b in (1, 0):
+            k, rows, _ = half(j, b)
+            for d in range(2):
+                arrive(radj.at[h, d, k, rows], a_recv.at[h, d, j, b])
+            part[h, 3, k, rows] = part[h, 3, k, rows] + (radj[h, 0, k, rows] + radj[h, 1, k, rows])
+            if j == 0:
+                remote(part.at[h, 3, 0, rows], rx.at[h, rows], s_send.at[2 + h], x_recv.at[h, b], XL)
+
+    def sums_start(h):
+        first_x(h)
+        now(h, 0)
+        now(h, 1)
+        for yo in range(4):
+            emit(h, yo, 1, range(FY // 128, 4))
+        for j in range(2):
+            emit(h, 3, j, range(FY // 128))
+
+    def final(h):
+        for b in range(2):
+            _, rows, _ = half(0, b)
+            arrive(rx.at[h, rows], x_recv.at[h, b])
+            part[h, 3, 1, rows] = part[h, 3, 1, rows] + rx[h, rows]
+        for u in range(4):
             rr = pl.ds(u * 128, 128)
-            v = part[h, 3, 1, rr] + rx[h, rr]
+            v = part[h, 3, 1, rr]
             hi = v.astype(BF16)
             lo = (v - hi.astype(F32)).astype(BF16)
             m = (jnp.dot(hi, wb[h, 0], preferred_element_type=F32)
@@ -278,9 +316,9 @@
                 return 0
             lax.fori_loop(0, 8, take, 0)
         pack(0, u)
-        if u == 0:
-            pl.semaphore_wait(barrier, len(around))
-        own_sends(0, u)
+    pl.semaphore_wait(barrier, len(around))
+    start(0)
+    more(0)
     ivec[...] = jnp.zeros_like(ivec)
     fvec[...] = jnp.zeros_like(fvec)
     tables()
@@ -295,15 +333,24 @@
             if p is not None:
                 a_piece(p)
 
-    a_pieces(2)
+    a_pieces(1)
     relay(0, 0)
-    a_pieces(2)
+    a_pieces(1)
+    relay(0, 2)
+    fill(0, 0)
+    a_pieces(1)
     across(0, 0)
-    relay(0, 2)
-    a_pieces(2)
-    for b in range(1, NB):
-        across(0, b)
+    fill(0, 2)
+    a_pieces(1)
+    across(0, 1)
+    a_pieces(1)
+    for b in range(NB):
+        stage2(0, b)
         a_pieces(1)
+    across(0, 2)
+    a_pieces(1)
+    across(0, 3)
+    a_pieces(1)
     for u in range(4):
         pack(1, u)
     for h in range(2):
@@ -318,16 +365,15 @@
     for b in (0, 2):
         rest(0, b)
         a_pieces(1)
-    for b in range(NB):
-        stage2(0, b)
-        a_pieces(1)
     for s in (P0, AM, AP, A2):
         convert(0, s)
         a_pieces(1)
+    start(1)
     for b in range(NB):
         stage2b(0, b)
-        own_sends(1, b)
         a_pieces(1)
+    more(1)
+    a_pieces(T // APIECE)
     for s in (BM, BP):
         convert(0, s)
     for b in range(NB):
@@ -345,20 +391,12 @@
 
     compute(0, {
         0: both((relay, 1, 0)),
-        1: both((across, 1, 0), (relay, 1, 2)),
-        2: both((across, 1, 1)),
-        3: both((across, 1, 2), (rest, 1, 0)),
+        1: both((relay, 1, 2), (fill, 1, 0), (across, 1, 0), (fill, 1, 2)),
+        2: both((across, 1, 1), (stage2, 1, 0), (stage2, 1, 1)),
+        3: both((stage2, 1, 2), (stage2, 1, 3), (across, 1, 2), (rest, 1, 0)),
         4: both((across, 1, 3), (rest, 1, 2)),
     })
-    for j in range(2):
-        opp(0, j)
-        adj_now(0, j)
-    for b in range(NB):
-        stage2(1, b)
-    for j in range(2):
-        adj_late(0, j)
-    for j in range(2):
-        emit(0, 3, j)
+    sums_start(0)
     for s in (P0, AM, AP, A2):
         convert(1, s)
     for b in range(NB):
@@ -371,31 +409,26 @@
     stage4(1)
 
     compute(1, {
-        3: both((own_sum, 0, 0, 1)),
-        4: both((own_sum, 0, 0, 0)),
+        0: both((adj_late, 0, 0), (first_add, 0)),
+        1: both((adj_late, 0, 1)),
+        2: both((adj_late, 0, 2)),
+        4: both((own_sum, 0, 0)),
     })
-    opp(1, 0)
-    adj_now(1, 0)
-    opp(1, 1)
-    adj_now(1, 1)
-    emit(1, 3, 0)
-    emit(1, 3, 1)
-    for b in (1, 0):
-        own_sum(0, 1, b)
+    sums_start(1)
     adj_late(1, 0)
-    for b in (1, 0):
-        final(0, b)
+    own_sum(0, 1)
+    first_add(1)
     adj_late(1, 1)
-    for j in range(2):
-        for b in (1, 0):
-            own_sum(1, j, b)
-    for b in (1, 0):
-        final(1, b)
-    for make in sends:
-        make().wait_send()
-
-
-N_SEND = 2 * (15 * NB + 14)
+    own_sum(0, 2)
+    final(0)
+    own_sum(1, 0)
+    adj_late(1, 2)
+    own_sum(1, 1)
+    own_sum(1, 2)
+    final(1)
+    for h in range(2):
+        sent(recv.at[0, pl.ds(0, 15)], s_send.at[h])
+        sent(recv.at[0, pl.ds(0, 7)], s_send.at[2 + h])
 
 
 def shards(features, weight, adjacency_tiles, tile_rows, tile_cols, tile_counts, cluster_order):
@@ -426,7 +459,8 @@
             pltpu.VMEM((ASTAGE, APIECE, 128, 128), F32),
             pltpu.VMEM((T // 2, 128, 128), F32),
             pltpu.VMEM((2, 4, 2, 512, 128), F32),
-            pltpu.VMEM((2, 2, 2, 256, 128), F32),
+            pltpu.VMEM((2, 4, 512 - FY, 128), F32),
+            pltpu.VMEM((2, 2, 3, FY // 2, 128), F32),
             pltpu.VMEM((2, 2, 2, 512, 128), F32),
             pltpu.VMEM((2, 512, 128), F32),
             pltpu.VMEM((1024, 128), F32),
@@ -435,10 +469,12 @@
             pltpu.VMEM((16, 128), F32),
             pltpu.SMEM((16, 128), jnp.int32),
             pltpu.SMEM((16, 128), F32),
-            dma((2, 16, NB)),
-            dma((N_SEND,)),
-            dma((2, 2, 2)),
-            dma((2, 2, 2, 2)),
+            dma((2, 8, NB)),
+            dma((2, 8)),
+            dma((4,)),
+            dma((2,)),
+            dma((2, 2, 3)),
+            dma((2, 2, 3, 2)),
             dma((2, 2)),
             dma((ASTAGE,)),
             dma((2,)),

time: 87.4 us -> 81 us (0.927); the launches traced: 87.1 us -> 79.7 us
  Pallas kernels: 83.2 us -> 75.8 us
    pallas_call x1, Pallas kernels: 83.2 us -> 75.8 us  [shards(): pl.pallas_call(body, out_shape=jax.ShapeDtypeStruct((1024, 128), F32), in...]
where the time goes in v3:
time: 81 us; the launch traced here: 79.7 us
  Pallas kernels  75.8 us (94%)
  local copies, waits for them, and re-layouts  1.87 us (2%)
  other arithmetic  1.39 us (2%)
    pallas_call x1, Pallas kernels, shards(): pl.pallas_call(body, out_shape=jax.ShapeDtypeStruct((1024, 128), F32), in...  75.8 us
    unnamed x1, local copies, waits for them, and re-layouts  1.87 us

profile of v3, /device:TPU:0, one launch (start us, length us, event | category | flops | bytes accessed | tf_op | source)
XLA Modules:
  0.0 79.7 jit_solution(453063222796236995)
XLA Ops:
  0.7 0.7 fusion.12
  1.4 0.7 add_bitcast_fusion.code
  2.0 75.8 %shard_map.73 = f32[1024,128]{1,0:T(8,128)} custom-call(s32[1,1024]{1,0:T(1,128)} %order.1, s32[3,128]{1,0:T(4,128)} %add_bitcast_fusion.code, f32[1024,128]{1,0:T(8,128)} %feat.1, f32[128,128]{1,0:T(8,128)} %weight.1, f32[320,128,128]{2,1,0:T(8,128)} %adj.1), custom_call_target="tpu_custom_call" | custom-call | tf_op jit(solution)/shard_map/pallas_call | solution.py:450
  77.8 1.9 %copy.10 = f32[1024,128]{1,0:T(8,128)} copy(f32[1024,128]{1,0:T(8,128)} %shard_map.73) | data formatting | bytes 1048576
  (1 shorter events, 0.0 us)

commit v4 on v3

--- a/solution.py
+++ b/solution.py
@@ -227,8 +227,6 @@
         return min(j, 1), pl.ds((FY if j == 2 else 0) + b * n, n), pl.ds(0, n)
 
     def first_x(h):
-        for yo in range(4):
-            emit(h, yo, 0, range(FY // 128, 4))
         remote(part.at[h, :, 0, LATE], first.at[h], s_send.at[2 + h], f_recv.at[h], XL)
 
     def first_add(h):
@@ -271,7 +269,10 @@
                 remote(part.at[h, 3, 0, rows], rx.at[h, rows], s_send.at[2 + h], x_recv.at[h, b], XL)
 
     def sums_start(h):
-        first_x(h)
+        for yo in range(4):
+            emit(h, yo, 0, range(FY // 128, 4))
+        if h == 1:
+            first_x(h)
         now(h, 0)
         now(h, 1)
         for yo in range(4):
@@ -381,6 +382,7 @@
     convert(0, B2)
     for copy in table_copies():
         copy.wait()
+    fill(1, 0)
     stage4(0)
 
     def both(*runs):
@@ -390,8 +392,8 @@
         return go
 
     compute(0, {
-        0: both((relay, 1, 0)),
-        1: both((relay, 1, 2), (fill, 1, 0), (across, 1, 0), (fill, 1, 2)),
+        0: both((relay, 1, 0), (relay, 1, 2)),
+        1: both((fill, 1, 2), (across, 1, 0)),
         2: both((across, 1, 1), (stage2, 1, 0), (stage2, 1, 1)),
         3: both((stage2, 1, 2), (stage2, 1, 3), (across, 1, 2), (rest, 1, 0)),
         4: both((across, 1, 3), (rest, 1, 2)),
@@ -401,18 +403,20 @@
         convert(1, s)
     for b in range(NB):
         stage2b(1, b)
+    for b in range(NB):
+        stage3(1, b)
+    first_x(0)
     for s in (BM, BP):
         convert(1, s)
-    for b in range(NB):
-        stage3(1, b)
     convert(1, B2)
     stage4(1)
 
     compute(1, {
-        0: both((adj_late, 0, 0), (first_add, 0)),
+        0: both((adj_late, 0, 0)),
         1: both((adj_late, 0, 1)),
-        2: both((adj_late, 0, 2)),
-        4: both((own_sum, 0, 0)),
+        2: both((first_add, 0)),
+        3: both((own_sum, 0, 0)),
+        4: both((adj_late, 0, 2)),
     })
     sums_start(1)
     adj_late(1, 0)

time: 81 us -> 77.5 us (0.957); the launches traced: 79.7 us -> 77.3 us
  Pallas kernels: 75.8 us -> 73.4 us
    pallas_call x1, Pallas kernels: 75.8 us -> 73.4 us  [shards(): pl.pallas_call(body, out_shape=jax.ShapeDtypeStruct((1024, 128), F32), in...]
where the time goes in v4:
time: 77.5 us; the launch traced here: 77.3 us
  Pallas kernels  73.4 us (95%)
  local copies, waits for them, and re-layouts  1.87 us (2%)
  other arithmetic  1.39 us (2%)
    pallas_call x1, Pallas kernels, shards(): pl.pallas_call(body, out_shape=jax.ShapeDtypeStruct((1024, 128), F32), in...  73.4 us
    unnamed x1, local copies, waits for them, and re-layouts  1.87 us

profile of v4, /device:TPU:0, one launch (start us, length us, event | category | flops | bytes accessed | tf_op | source)
XLA Modules:
  0.0 77.3 jit_solution(9205232911629827223)
XLA Ops:
  0.7 0.7 fusion.12
  1.4 0.7 add_bitcast_fusion.code
  2.0 73.4 %shard_map.73 = f32[1024,128]{1,0:T(8,128)} custom-call(s32[1,1024]{1,0:T(1,128)} %order.1, s32[3,128]{1,0:T(4,128)} %add_bitcast_fusion.code, f32[1024,128]{1,0:T(8,128)} %feat.1, f32[128,128]{1,0:T(8,128)} %weight.1, f32[320,128,128]{2,1,0:T(8,128)} %adj.1), custom_call_target="tpu_custom_call" | custom-call | tf_op jit(solution)/shard_map/pallas_call | solution.py:454
  75.4 1.9 %copy.10 = f32[1024,128]{1,0:T(8,128)} copy(f32[1024,128]{1,0:T(8,128)} %shard_map.73) | data formatting | bytes 1048576
  (1 shorter events, 0.0 us)

commit v5 on v4

--- a/solution.py
+++ b/solution.py
@@ -319,6 +319,7 @@
         pack(0, u)
     pl.semaphore_wait(barrier, len(around))
     start(0)
+    fill(0, 0)
     more(0)
     ivec[...] = jnp.zeros_like(ivec)
     fvec[...] = jnp.zeros_like(fvec)
@@ -338,7 +339,6 @@
     relay(0, 0)
     a_pieces(1)
     relay(0, 2)
-    fill(0, 0)
     a_pieces(1)
     across(0, 0)
     fill(0, 2)
@@ -438,16 +438,15 @@
 def shards(features, weight, adjacency_tiles, tile_rows, tile_cols, tile_counts, cluster_order):
     c = lax.axis_index("rep")
     y, xl = c // 2, c % 2
-    j = jnp.arange(T, dtype=jnp.int32)
+    j = jnp.arange(384, dtype=jnp.int32)
+    tile_rows, tile_cols = (jnp.pad(v, (0, 384 - T)) for v in (tile_rows, tile_cols))
     dy, rx_, t = (tile_rows // 16 - y) % 4, (tile_rows // 8) % 2, tile_rows % 8
     yo = jnp.where(dy == 0, 3, jnp.where(dy == 1, 1, jnp.where(dy == 2, 0, 2)))
     rel = ((yo * 2 + (rx_ == xl)) * 4 + t % 4) * 2 + t // 4
     key = jnp.where(j < tile_counts[0], rel, 64)
     k, o = tile_cols // 8, tile_cols % 8
     panel = ((k % 2) * 8 + k // 2) * 4 + o % 4
-    code = key * 65536 + (o // 4) * 32768 + panel * 512 + j
-    more = jnp.arange(T, 384, dtype=jnp.int32) + 64 * 65536
-    code = jnp.concatenate([code, more]).reshape(3, 128)
+    code = (key * 65536 + (o // 4) * 32768 + panel * 512 + j).reshape(3, 128)
     smem = pl.BlockSpec(memory_space=pltpu.SMEM)
     vmem = pl.BlockSpec(memory_space=pltpu.VMEM)
     dma = pltpu.SemaphoreType.DMA

time: 77.5 us -> 75.6 us (0.975)
  Pallas kernels: 73.4 us -> 71 us
    pallas_call x1, Pallas kernels: 73.4 us -> 71 us  [shards(): pl.pallas_call(body, out_shape=jax.ShapeDtypeStruct((1024, 128), F32), in...]
where the time goes in v5:
time: 75.6 us; the launch traced here: 74.9 us
  Pallas kernels  71 us (94%)
  local copies, waits for them, and re-layouts  1.87 us (2%)
  other arithmetic  1.31 us (2%)
    pallas_call x1, Pallas kernels, shards(): pl.pallas_call(body, out_shape=jax.ShapeDtypeStruct((1024, 128), F32), in...  71 us
    unnamed x1, local copies, waits for them, and re-layouts  1.87 us

profile of v5, /device:TPU:0, one launch (start us, length us, event | category | flops | bytes accessed | tf_op | source)
XLA Modules:
  0.0 74.9 jit_solution(15666701038654196304)
XLA Ops:
  0.7 1.3 %fusion.27.code = s32[3,128]{1,0:T(4,128)} fusion(s32[320]{0:T(512)} %param.11, s32[320]{0:T(512)} %param.10, s32[]{:T(128)S(6)} %select_n.84, s32[]{:T(128)S(6)} %select_n.77, s32[]{:T(128)} %bitcast.3), kind=kLoop, calls=%fused_computation.67 | loop fusion | flops 59136 | bytes 4108 | tf_op jit(solution)/shard_map/reshape | solution.py:449
  2.0 71.0 %shard_map.73 = f32[1024,128]{1,0:T(8,128)} custom-call(s32[1,1024]{1,0:T(1,128)} %order.1, s32[3,128]{1,0:T(4,128)} %fusion.27.code, f32[1024,128]{1,0:T(8,128)} %feat.1, f32[128,128]{1,0:T(8,128)} %weight.1, f32[320,128,128]{2,1,0:T(8,128)} %adj.1), custom_call_target="tpu_custom_call" | custom-call | tf_op jit(solution)/shard_map/pallas_call | solution.py:453
  73.0 1.9 %copy.10 = f32[1024,128]{1,0:T(8,128)} copy(f32[1024,128]{1,0:T(8,128)} %shard_map.73) | data formatting | bytes 1048576
